TPU v7x, 32 devices: a whole 2x2x4 slice. The times are simulated.
32 devices in a mesh: ja: 4 (over x, core), ka: 8 (over z, y).
Axes of the slice: x: 2, y: 2, z: 4, core: 2. Of those that a mesh axis runs over, the one named last changes fastest.
Arguments:
- conserved: float32 [5, 128, 64, 128], P(None, 'ja', 'ka'), may hold values from -2 to 6.5, as said below
- blanking: int32 [128, 64, 128], P('ja', 'ka'), may hold values 0 or 1
- wall_type: int32 [128, 128], P('ja'), may hold values from 0 to 2
- char_around: float32 [5, 5], replicated, may hold values from -0.5 to 2.5
- around_to_axial: float32 [5, 5], replicated, may hold values from -0.5 to 2.5
- axial_to_normal: float32 [5, 5], replicated, may hold values from -0.5 to 2.5
- char_back: float32 [5, 5], replicated, may hold values from -0.5 to 2.5
- around_inverse: float32 [5, 128, 128], replicated, may hold values from 0 to 2
- axial_inverse: float32 [5, 128, 128], replicated, may hold values from 0 to 2
- normal_inverse: float32 [5, 64, 64], replicated, may hold values from 0 to 2
Outputs:
- right_side: float32 [5, 128, 64, 128], P(None, 'ja', 'ka')
- update: float32 [5, 128, 64, 128], P(None, 'ja', 'ka')
Inputs may be any that keep to these rules, and one draw needn't show every extreme that they name: `conserved`: component 0, the density, is 0.5 or more in every cell.
All inputs are finite; a program needn't handle non-finite values. No bound on the sum of `blanking` on one device may be relied on, other than what follows from the above.
Results may differ from a plain program's by a relative error of at most 0.00019.
Values sent between devices are 32-bit elements; how exact they have to be, the bound alone decides.
A program may use at most 64 MiB of HBM per device.

v0:
```python
import functools

import jax
import jax.numpy as jnp
from jax import lax
from jax.experimental import pallas as pl
from jax.experimental.pallas import tpu as pltpu
from jax.sharding import PartitionSpec as P

F32 = jnp.float32
BF16 = jnp.bfloat16
MESH = pl.DeviceIdType.MESH
FREESTREAM = (1.0, 0.4, 0.1, 0.0, 2.585)
TOP = 8


def flux(state, direction):
    inverse = 1.0 / state[0]
    kinetic = state[1] * state[1] + state[2] * state[2] + state[3] * state[3]
    pressure = 0.4 * (state[4] - 0.5 * kinetic * inverse)
    velocity = state[direction] * inverse
    pieces = [state[direction]]
    for member in (1, 2, 3):
        piece = state[member] * velocity
        pieces.append(piece + pressure if member == direction else piece)
    pieces.append((state[4] + pressure) * velocity)
    return pieces


def mix(matrix, values):
    out = []
    for a in range(5):
        total = matrix[a, 0] * values[0]
        for b in range(1, 5):
            total = total + matrix[a, b] * values[b]
        out.append(total)
    return out


def halves(x):
    high = x.astype(BF16)
    return high, (x - high.astype(F32)).astype(BF16)


def dot(x, y, dims):
    return lax.dot_general(x, y, (dims, ((), ())), preferred_element_type=F32)


def kernel(
    nja,
    nka,
    cells,
    blanking,
    wall,
    char_around,
    around_to_axial,
    axial_to_normal,
    char_back,
    around_inverse,
    axial_inverse,
    normal_inverse,
    right_side,
    update,
    q,
    jhalo,
    first,
    asend,
    x,
    solved,
    bsend,
    y,
    w,
    z,
    normal,
    csend,
    u,
    around3,
    axial3,
    normal3,
    jsem,
    ksem,
    a_send,
    a_recv,
    b_send,
    b_recv,
    w_send,
    w_recv,
    c_send,
    c_recv,
):
    cj = wall.shape[0]
    ck = cells.shape[1] // cj
    ni = cells.shape[2]
    kp = ck // nja
    jq = cj // nka
    mj = lax.axis_index("ja")
    mk = lax.axis_index("ka")

    barrier = pltpu.get_barrier_semaphore()
    for o in range(1, nja):
        pl.semaphore_signal(
            barrier, inc=1, device_id={"ja": lax.rem(mj + o, nja)}, device_id_type=MESH
        )
    for o in range(1, nka):
        pl.semaphore_signal(
            barrier, inc=1, device_id={"ka": lax.rem(mk + o, nka)}, device_id_type=MESH
        )

    def spread(k, carry):
        for c in range(5):
            q[c, k + 2, TOP : TOP + cj, :] = cells[c, pl.ds(k, cj, stride=ck), :]
        return carry

    lax.fori_loop(0, ck, spread, 0)
    pl.semaphore_wait(barrier, nja - 1 + nka - 1)

    def khalo(upward):
        if upward:
            src, dst, other = ck, 0, mk + 1
        else:
            src, dst, other = 2, ck + 2, mk - 1
        return pltpu.make_async_remote_copy(
            src_ref=q.at[:, src : src + 2, TOP : TOP + cj, :],
            dst_ref=q.at[:, dst : dst + 2, TOP : TOP + cj, :],
            send_sem=ksem.at[0, int(upward)],
            recv_sem=ksem.at[1, int(upward)],
            device_id={"ka": other},
            device_id_type=MESH,
        )

    def jhalo_copy(upward):
        if upward:
            src, dst, other = (cj - 2) * ck, 0, mj + 1
        else:
            src, dst, other = 0, 1, mj - 1
        return pltpu.make_async_remote_copy(
            src_ref=cells.at[:, src : src + 2 * ck, :],
            dst_ref=jhalo.at[dst],
            send_sem=jsem.at[0, int(upward)],
            recv_sem=jsem.at[1, int(upward)],
            device_id={"ja": other},
            device_id_type=MESH,
        )

    @pl.when(mj < nja - 1)
    def _():
        jhalo_copy(True).start()

    @pl.when(mj > 0)
    def _():
        jhalo_copy(False).start()

    @pl.when(mk < nka - 1)
    def _():
        khalo(True).start()

    @pl.when(mk > 0)
    def _():
        khalo(False).start()

    @pl.when(mj == 0)
    def _():
        for c in range(5):
            jhalo[0, c] = jnp.full((2 * ck, ni), FREESTREAM[c], F32)

    @pl.when(mj == nja - 1)
    def _():
        for c in range(5):
            jhalo[1, c] = jnp.full((2 * ck, ni), FREESTREAM[c], F32)

    @pl.when(mk == 0)
    def _():
        kind = wall[...]
        for c in range(5):
            near = q[c, 2, TOP : TOP + cj, :]
            far = q[c, 3, TOP : TOP + cj, :]
            sign = -1.0 if c == 3 else 1.0
            rest = jnp.where(kind == 1, near, FREESTREAM[c])
            q[c, 1, TOP : TOP + cj, :] = jnp.where(kind == 0, sign * near, rest)
            q[c, 0, TOP : TOP + cj, :] = jnp.where(kind == 0, sign * far, rest)

    @pl.when(mk == nka - 1)
    def _():
        for c in range(5):
            for r in range(2):
                q[c, ck + 2 + r, TOP : TOP + cj, :] = jnp.full((cj, ni), FREESTREAM[c], F32)

    for c in range(5):
        high, low = halves(around_inverse[c])
        around3[c] = jnp.concatenate([high, low, high], axis=1)
        high, low = halves(axial_inverse[c])
        axial3[c] = jnp.concatenate([high, high, low], axis=1)
        high, low = halves(normal_inverse[c])
        normal3[c] = jnp.concatenate([high, high, low], axis=1)

    @pl.when(mj > 0)
    def _():
        jhalo_copy(True).wait_recv()

    @pl.when(mj < nja - 1)
    def _():
        jhalo_copy(False).wait_recv()

    def plane(k, carry):
        at = k + 2
        for c in range(5):
            for r in range(2):
                row = pl.ds(r * ck + k, 1)
                q[c, at, TOP - 2 + r : TOP - 1 + r, :] = jhalo[0, c, row, :]
                q[c, at, TOP + cj + r : TOP + cj + r + 1, :] = jhalo[1, c, row, :]

        def rows(offset):
            return [q[c, at, TOP + offset : TOP + offset + cj, :] for c in range(5)]

        def layer(offset):
            return [q[c, at + offset, TOP : TOP + cj, :] for c in range(5)]

        here = rows(0)
        flow = flux(here, 1)
        total = []
        for c in range(5):
            plus = 0.5 * flow[c] - 0.375 * here[c]
            minus = -0.5 * flow[c] - 0.375 * here[c]
            wide = pltpu.roll(here[c], 2, 1) + pltpu.roll(here[c], ni - 2, 1)
            total.append(
                2.0625 * here[c]
                + pltpu.roll(plus, ni - 1, 1)
                + pltpu.roll(minus, 1, 1)
                + wide * (1.0 / 32.0)
            )
        for direction, reader in ((2, rows), (3, layer)):
            above, below = reader(1), reader(-1)
            top, bottom = flux(above, direction), flux(below, direction)
            for c in range(5):
                total[c] = total[c] + 0.5 * (top[c] - bottom[c]) - 0.375 * (above[c] + below[c])
            above, below = reader(2), reader(-2)
            for c in range(5):
                total[c] = total[c] + (above[c] + below[c]) * (1.0 / 32.0)
        weight = -0.5 * blanking[pl.ds(k, cj, stride=ck), :].astype(F32)
        total = [t * weight for t in total]
        for c in range(5):
            right_side[c, pl.ds(k, cj, stride=ck), :] = total[c]
        mixed = mix(char_around, total)
        for c in range(5):
            first[c, k] = mixed[c]
        return carry

    def a_copy(dest):
        return pltpu.make_async_remote_copy(
            src_ref=asend.at[dest],
            dst_ref=x.at[:, :, pl.ds(pl.multiple_of(mj * cj, 8), cj), :],
            send_sem=a_send.at[dest],
            recv_sem=a_recv.at[mj],
            device_id={"ja": dest},
            device_id_type=MESH,
        )

    def around(start, count):
        out = []
        for c in range(5):
            high, low = halves(first[c, start : start + count].reshape(count * cj, ni))
            out.append(
                dot(jnp.concatenate([high, high, low], axis=1), around3[c], ((1,), (1,)))
            )
        out = mix(around_to_axial, out)
        for c in range(5):
            for s in range(count):
                k = start + s
                asend[k // kp, c, k % kp] = out[c][s * cj : (s + 1) * cj]
        for dest in range(start // kp, (start + count) // kp):

            @pl.when(dest != mj)
            def _():
                a_copy(dest).start()

    edge = 2
    lax.fori_loop(edge, ck - edge, plane, 0)
    around(edge, ck - 2 * edge)

    @pl.when(mk > 0)
    def _():
        khalo(True).wait_recv()

    @pl.when(mk < nka - 1)
    def _():
        khalo(False).wait_recv()

    lax.fori_loop(0, edge, plane, 0)
    around(0, edge)
    lax.fori_loop(ck - edge, ck, plane, 0)
    around(ck - edge, edge)

    own = pl.ds(pl.multiple_of(mj * cj, 8), cj)
    for c in range(5):
        for s in range(kp):
            x[c, s, own, :] = asend[mj, c, s]

    for o in range(1, nja):
        source = lax.rem(mj + o, nja)
        pltpu.make_async_remote_copy(
            src_ref=asend.at[source],
            dst_ref=x.at[:, :, pl.ds(pl.multiple_of(source * cj, 8), cj), :],
            send_sem=a_send.at[source],
            recv_sem=a_recv.at[source],
            device_id={"ja": source},
            device_id_type=MESH,
        ).wait_recv()

    for c in range(5):
        high, low = halves(jnp.concatenate([x[c, s] for s in range(kp)], axis=1))
        out = dot(axial3[c], jnp.concatenate([high, low, high], axis=0), ((1,), (0,)))
        for s in range(kp):
            solved[c, s] = out[:, s * ni : (s + 1) * ni]

    def b_copy(dest, source):
        return pltpu.make_async_remote_copy(
            src_ref=bsend.at[dest],
            dst_ref=y.at[:, pl.ds(pl.multiple_of(source * (kp * cj), 8), kp * cj), :],
            send_sem=b_send.at[dest],
            recv_sem=b_recv.at[source],
            device_id={"ja": dest},
            device_id_type=MESH,
        )

    for o in range(1, nja + 1):
        dest = lax.rem(mj + o, nja)
        for s in range(kp):
            block = [
                solved[c, s, pl.ds(pl.multiple_of(dest * cj, 8), cj), :] for c in range(5)
            ]
            block = mix(axial_to_normal, block)
            for c in range(5):
                if o < nja:
                    bsend[dest, c, s * cj : (s + 1) * cj, :] = block[c]
                else:
                    y[c, pl.ds(pl.multiple_of((mj * kp + s) * cj, 8), cj), :] = block[c]
        if o < nja:
            b_copy(dest, mj).start()
    for o in range(1, nja):
        source = lax.rem(mj + o, nja)
        b_copy(source, source).wait_recv()

    def w_copy(dest, source):
        return pltpu.make_async_remote_copy(
            src_ref=w.at[dest],
            dst_ref=z.at[:, :, pl.ds(pl.multiple_of(source * ck, 8), ck), :],
            send_sem=w_send.at[dest],
            recv_sem=w_recv.at[source],
            device_id={"ka": dest},
            device_id_type=MESH,
        )

    for o in range(1, nka + 1):
        dest = lax.rem(mk + o, nka)
        for s in range(jq):
            for c in range(5):
                tile = y[c, pl.ds(dest * jq + s, ck, stride=cj), :]
                if o < nka:
                    w[dest, c, s] = tile
                else:
                    z[c, s, pl.ds(pl.multiple_of(mk * ck, 8), ck), :] = tile
        if o < nka:
            w_copy(dest, mk).start()
    for o in range(1, nka):
        source = lax.rem(mk + o, nka)
        w_copy(source, source).wait_recv()

    for c in range(5):
        high, low = halves(jnp.concatenate([z[c, s] for s in range(jq)], axis=1))
        out = dot(normal3[c], jnp.concatenate([high, low, high], axis=0), ((1,), (0,)))
        for s in range(jq):
            normal[c, s] = out[:, s * ni : (s + 1) * ni]

    def c_copy(dest, source):
        return pltpu.make_async_remote_copy(
            src_ref=csend.at[dest],
            dst_ref=u.at[:, pl.ds(pl.multiple_of(source * (jq * ck), 8), jq * ck), :],
            send_sem=c_send.at[dest],
            recv_sem=c_recv.at[source],
            device_id={"ka": dest},
            device_id_type=MESH,
        )

    for o in range(1, nka + 1):
        dest = lax.rem(mk + o, nka)
        for s in range(jq):
            block = [
                normal[c, s, pl.ds(pl.multiple_of(dest * ck, 8), ck), :] for c in range(5)
            ]
            block = mix(char_back, block)
            for c in range(5):
                if o < nka:
                    csend[dest, c, s * ck : (s + 1) * ck, :] = block[c]
                else:
                    u[c, pl.ds(pl.multiple_of((mk * jq + s) * ck, 8), ck), :] = block[c]
        if o < nka:
            c_copy(dest, mk).start()
    for o in range(1, nka):
        source = lax.rem(mk + o, nka)
        c_copy(source, source).wait_recv()

    weight = blanking[...].astype(F32)
    for c in range(5):
        update[c] = u[c] * weight

    for upward, last, here in ((True, nja - 1, mj), (False, 0, mj)):

        @pl.when(here != last)
        def _(upward=upward):
            jhalo_copy(upward).wait_send()

    for upward, last, here in ((True, nka - 1, mk), (False, 0, mk)):

        @pl.when(here != last)
        def _(upward=upward):
            khalo(upward).wait_send()

    for o in range(1, nja):
        other = lax.rem(mj + o, nja)
        a_copy(other).wait_send()
        b_copy(other, mj).wait_send()
    for o in range(1, nka):
        other = lax.rem(mk + o, nka)
        w_copy(other, mk).wait_send()
        c_copy(other, mk).wait_send()


def body(
    conserved,
    blanking,
    wall_type,
    char_around,
    around_to_axial,
    axial_to_normal,
    char_back,
    around_inverse,
    axial_inverse,
    normal_inverse,
):
    nja = lax.axis_size("ja")
    nka = lax.axis_size("ka")
    _, cj, ck, ni = conserved.shape
    nj, nk = cj * nja, ck * nka
    kp, jq = ck // nja, cj // nka
    vmem = pl.BlockSpec(memory_space=pltpu.VMEM)
    smem = pl.BlockSpec(memory_space=pltpu.SMEM)
    flat = jax.ShapeDtypeStruct((5, cj * ck, ni), F32)
    dma = pltpu.SemaphoreType.DMA
    right_side, update = pl.pallas_call(
        functools.partial(kernel, nja, nka),
        out_shape=(flat, flat),
        in_specs=[vmem] * 3 + [smem] * 4 + [vmem] * 3,
        out_specs=(vmem, vmem),
        scratch_shapes=[
            pltpu.VMEM((5, ck + 4, cj + 16, ni), F32),
            pltpu.VMEM((2, 5, 2 * ck, ni), F32),
            pltpu.VMEM((5, ck, cj, ni), F32),
            pltpu.VMEM((nja, 5, kp, cj, ni), F32),
            pltpu.VMEM((5, kp, nj, ni), F32),
            pltpu.VMEM((5, kp, nj, ni), F32),
            pltpu.VMEM((nja, 5, kp * cj, ni), F32),
            pltpu.VMEM((5, ck * cj, ni), F32),
            pltpu.VMEM((nka, 5, jq, ck, ni), F32),
            pltpu.VMEM((5, jq, nk, ni), F32),
            pltpu.VMEM((5, jq, nk, ni), F32),
            pltpu.VMEM((nka, 5, jq * ck, ni), F32),
            pltpu.VMEM((5, cj * ck, ni), F32),
            pltpu.VMEM((5, ni, 3 * ni), BF16),
            pltpu.VMEM((5, nj, 3 * nj), BF16),
            pltpu.VMEM((5, nk, 3 * nk), BF16),
            dma((2, 2)),
            dma((2, 2)),
            dma((nja,)),
            dma((nja,)),
            dma((nja,)),
            dma((nja,)),
            dma((nka,)),
            dma((nka,)),
            dma((nka,)),
            dma((nka,)),
        ],
        compiler_params=pltpu.CompilerParams(
            collective_id=0, has_side_effects=True, vmem_limit_bytes=48 * 1024 * 1024
        ),
    )(
        conserved.reshape(5, cj * ck, ni),
        blanking.reshape(cj * ck, ni),
        wall_type,
        char_around,
        around_to_axial,
        axial_to_normal,
        char_back,
        around_inverse,
        axial_inverse,
        normal_inverse,
    )
    return right_side.reshape(conserved.shape), update.reshape(conserved.shape)


def solution(mesh):
    slabs = P(None, "ja", "ka", None)
    return jax.shard_map(
        body,
        mesh=mesh,
        in_specs=(slabs, P("ja", "ka", None), P("ja", None)) + (P(),) * 7,
        out_specs=(slabs, slabs),
        check_vma=False,
    )
```

profile of v0, /device:TPU:29, one launch (start us, length us, event | category | flops | bytes accessed | tf_op | source)
XLA Modules:
  0.0 67.6 jit_solution(16654992917758280175)
XLA Ops:
  0.6 0.0 copy-start
  0.6 1.1 %copy-done = f32[5,32,8,128]{3,2,1,0:T(8,128)S(1)} copy-done((f32[5,32,8,128]{3,2,1,0:T(8,128)S(1)}, f32[5,32,8,128]{3,2,1,0:T(8,128)}, u32[]{:S(2)}) %copy-start) | copy-done | bytes 655384
  1.7 0.0 copy-start.1
  1.7 1.0 %copy-done.1 = f32[5,128,128]{2,1,0:T(8,128)S(1)} copy-done((f32[5,128,128]{2,1,0:T(8,128)S(1)}, f32[5,128,128]{2,1,0:T(8,128)}, u32[]{:S(2)}) %copy-start.1) | copy-done | bytes 327704
  2.7 0.0 copy-start.2
  2.7 1.0 %copy-done.2 = f32[5,128,128]{2,1,0:T(8,128)S(1)} copy-done((f32[5,128,128]{2,1,0:T(8,128)S(1)}, f32[5,128,128]{2,1,0:T(8,128)}, u32[]{:S(2)}) %copy-start.2) | copy-done | bytes 327704
  3.7 0.0 copy-start.3
  3.7 0.9 %copy-done.3 = f32[5,64,64]{2,1,0:T(8,128)S(1)} copy-done((f32[5,64,64]{2,1,0:T(8,128)S(1)}, f32[5,64,64]{2,1,0:T(8,128)}, u32[]{:S(2)}) %copy-start.3) | copy-done | bytes 81944
  4.6 0.0 copy-start.4
  4.6 0.9 %copy-done.4 = s32[32,8,128]{2,1,0:T(8,128)S(1)} copy-done((s32[32,8,128]{2,1,0:T(8,128)S(1)}, s32[32,8,128]{2,1,0:T(8,128)}, u32[]{:S(2)}) %copy-start.4) | copy-done | bytes 131096
  5.5 0.0 copy-start.5
  5.5 0.7 %copy-done.5 = s32[32,128]{1,0:T(8,128)S(1)} copy-done((s32[32,128]{1,0:T(8,128)S(1)}, s32[32,128]{1,0:T(8,128)}, u32[]{:S(2)}) %copy-start.5) | copy-done | bytes 16408
  6.2 0.0 copy-start.6
  6.2 0.7 %copy-done.6 = f32[5,5]{1,0:T(8,128)S(1)} copy-done((f32[5,5]{1,0:T(8,128)S(1)}, f32[5,5]{1,0:T(8,128)}, u32[]{:S(2)}) %copy-start.6) | copy-done | bytes 124
  6.9 0.0 copy-start.7
  6.9 0.7 %copy-done.7 = f32[5,5]{1,0:T(8,128)S(1)} copy-done((f32[5,5]{1,0:T(8,128)S(1)}, f32[5,5]{1,0:T(8,128)}, u32[]{:S(2)}) %copy-start.7) | copy-done | bytes 124
  7.6 0.0 copy-start.8
  7.6 0.7 %copy-done.8 = f32[5,5]{1,0:T(8,128)S(1)} copy-done((f32[5,5]{1,0:T(8,128)S(1)}, f32[5,5]{1,0:T(8,128)}, u32[]{:S(2)}) %copy-start.8) | copy-done | bytes 124
  8.3 0.0 copy-start.9
  8.3 0.7 %copy-done.9 = f32[5,5]{1,0:T(8,128)S(1)} copy-done((f32[5,5]{1,0:T(8,128)S(1)}, f32[5,5]{1,0:T(8,128)}, u32[]{:S(2)}) %copy-start.9) | copy-done | bytes 124
  9.0 57.0 %shard_map.113 = (f32[5,256,128]{2,1,0:T(8,128)S(1)}, f32[5,256,128]{2,1,0:T(8,128)S(1)}) custom-call(f32[5,256,128]{2,1,0:T(8,128)S(1)} %bitcast.4, s32[256,128]{1,0:T(8,128)S(1)} %bitcast.7, s32[32,128]{1,0:T(8,128)S(1)} %copy-done.5, f32[5,5]{1,0:T(8,128)S(1)} %copy-done.6, f32[5,5]{1,0:T(8,128)S(1)} %copy-done.7, f32[5,5]{1,0:T(8,128)S(1)} %copy-done.8, ...), custom_call_target="tpu_custom_call" | custom-call | tf_op jit(solution)/shard_map/pallas_call | solution.py:449
  65.9 0.8 %copy.14 = f32[5,32,8,128]{3,2,1,0:T(8,128)} copy(f32[5,32,8,128]{3,2,1,0:T(8,128)S(1)} %bitcast.6) | data formatting | bytes 1310720
  66.8 0.8 %copy.15 = f32[5,32,8,128]{3,2,1,0:T(8,128)} copy(f32[5,32,8,128]{3,2,1,0:T(8,128)S(1)} %bitcast.5) | data formatting | bytes 1310720
Async XLA Ops:
  0.6 1.1 %copy-start = (f32[5,32,8,128]{3,2,1,0:T(8,128)S(1)}, f32[5,32,8,128]{3,2,1,0:T(8,128)}, u32[]{:S(2)}) copy-start(f32[5,32,8,128]{3,2,1,0:T(8,128)} %param.10) | copy-start | bytes 1966084
  1.7 1.0 %copy-start.1 = (f32[5,128,128]{2,1,0:T(8,128)S(1)}, f32[5,128,128]{2,1,0:T(8,128)}, u32[]{:S(2)}) copy-start(f32[5,128,128]{2,1,0:T(8,128)} %around_inverse.1) | copy-start | bytes 983044
  2.7 1.0 %copy-start.2 = (f32[5,128,128]{2,1,0:T(8,128)S(1)}, f32[5,128,128]{2,1,0:T(8,128)}, u32[]{:S(2)}) copy-start(f32[5,128,128]{2,1,0:T(8,128)} %axial_inverse.1) | copy-start | bytes 983044
  3.7 0.9 %copy-start.3 = (f32[5,64,64]{2,1,0:T(8,128)S(1)}, f32[5,64,64]{2,1,0:T(8,128)}, u32[]{:S(2)}) copy-start(f32[5,64,64]{2,1,0:T(8,128)} %normal_inverse.1) | copy-start | bytes 245764
  4.6 0.9 %copy-start.4 = (s32[32,8,128]{2,1,0:T(8,128)S(1)}, s32[32,8,128]{2,1,0:T(8,128)}, u32[]{:S(2)}) copy-start(s32[32,8,128]{2,1,0:T(8,128)} %param.11) | copy-start | bytes 393220
  5.5 0.7 %copy-start.5 = (s32[32,128]{1,0:T(8,128)S(1)}, s32[32,128]{1,0:T(8,128)}, u32[]{:S(2)}) copy-start(s32[32,128]{1,0:T(8,128)} %wall.1) | copy-start | bytes 49156
  6.2 0.7 %copy-start.6 = (f32[5,5]{1,0:T(8,128)S(1)}, f32[5,5]{1,0:T(8,128)}, u32[]{:S(2)}) copy-start(f32[5,5]{1,0:T(8,128)} %char_around.1) | copy-start | bytes 304
  6.9 0.7 %copy-start.7 = (f32[5,5]{1,0:T(8,128)S(1)}, f32[5,5]{1,0:T(8,128)}, u32[]{:S(2)}) copy-start(f32[5,5]{1,0:T(8,128)} %around_to_axial.1) | copy-start | bytes 304
  7.6 0.7 %copy-start.8 = (f32[5,5]{1,0:T(8,128)S(1)}, f32[5,5]{1,0:T(8,128)}, u32[]{:S(2)}) copy-start(f32[5,5]{1,0:T(8,128)} %axial_to_normal.1) | copy-start | bytes 304
  8.3 0.7 %copy-start.9 = (f32[5,5]{1,0:T(8,128)S(1)}, f32[5,5]{1,0:T(8,128)}, u32[]{:S(2)}) copy-start(f32[5,5]{1,0:T(8,128)} %char_back.1) | copy-start | bytes 304
where the time goes:
time: 68.1 us; the launch traced here: 67.6 us
  Pallas kernels  57 us (84%)
  local copies, waits for them, and re-layouts  9.98 us (15%)
    pallas_call x1, Pallas kernels, body(): pl.pallas_call(functools.partial(kernel, nja, nka), out_shape=(flat, flat...  57 us
    unnamed x22, local copies, waits for them, and re-layouts  9.98 us

commit v1 on v0

--- a/solution.py
+++ b/solution.py
@@ -49,18 +49,24 @@
 def kernel(
     nja,
     nka,
-    cells,
-    blanking,
-    wall,
-    char_around,
-    around_to_axial,
-    axial_to_normal,
-    char_back,
-    around_inverse,
-    axial_inverse,
-    normal_inverse,
-    right_side,
-    update,
+    *refs,
+):
+    sources, refs = refs[:10], refs[10:]
+    right_side, update = refs[:2]
+    inputs, refs = refs[2:12], refs[12:]
+    (
+        cells,
+        blanking,
+        wall,
+        char_around,
+        around_to_axial,
+        axial_to_normal,
+        char_back,
+        around_inverse,
+        axial_inverse,
+        normal_inverse,
+    ) = inputs
+    (
     q,
     jhalo,
     first,
@@ -87,7 +93,14 @@
     w_recv,
     c_send,
     c_recv,
-):
+        insem,
+    ) = refs
+    loads = [
+        pltpu.make_async_copy(source, held, insem.at[n])
+        for n, (source, held) in enumerate(zip(sources, inputs))
+    ]
+    for load in loads:
+        load.start()
     cj = wall.shape[0]
     ck = cells.shape[1] // cj
     ni = cells.shape[2]
@@ -105,6 +118,8 @@
         pl.semaphore_signal(
             barrier, inc=1, device_id={"ka": lax.rem(mk + o, nka)}, device_id_type=MESH
         )
+
+    loads[0].wait()
 
     def spread(k, carry):
         for c in range(5):
@@ -157,6 +172,9 @@
     @pl.when(mk > 0)
     def _():
         khalo(False).start()
+
+    for load in loads[1:]:
+        load.wait()
 
     @pl.when(mj == 0)
     def _():
@@ -443,15 +461,24 @@
     nj, nk = cj * nja, ck * nka
     kp, jq = ck // nja, cj // nka
     vmem = pl.BlockSpec(memory_space=pltpu.VMEM)
-    smem = pl.BlockSpec(memory_space=pltpu.SMEM)
     flat = jax.ShapeDtypeStruct((5, cj * ck, ni), F32)
     dma = pltpu.SemaphoreType.DMA
     right_side, update = pl.pallas_call(
         functools.partial(kernel, nja, nka),
         out_shape=(flat, flat),
-        in_specs=[vmem] * 3 + [smem] * 4 + [vmem] * 3,
+        in_specs=[pl.BlockSpec(memory_space=pltpu.HBM)] * 10,
         out_specs=(vmem, vmem),
         scratch_shapes=[
+            pltpu.VMEM((5, cj * ck, ni), F32),
+            pltpu.VMEM((cj * ck, ni), jnp.int32),
+            pltpu.VMEM((cj, ni), jnp.int32),
+            pltpu.SMEM((5, 5), F32),
+            pltpu.SMEM((5, 5), F32),
+            pltpu.SMEM((5, 5), F32),
+            pltpu.SMEM((5, 5), F32),
+            pltpu.VMEM((5, ni, ni), F32),
+            pltpu.VMEM((5, nj, nj), F32),
+            pltpu.VMEM((5, nk, nk), F32),
             pltpu.VMEM((5, ck + 4, cj + 16, ni), F32),
             pltpu.VMEM((2, 5, 2 * ck, ni), F32),
             pltpu.VMEM((5, ck, cj, ni), F32),
@@ -478,9 +505,10 @@
             dma((nka,)),
             dma((nka,)),
             dma((nka,)),
+            dma((10,)),
         ],
         compiler_params=pltpu.CompilerParams(
-            collective_id=0, has_side_effects=True, vmem_limit_bytes=48 * 1024 * 1024
+            collective_id=0, has_side_effects=True, vmem_limit_bytes=64 * 1024 * 1024 - 65536
         ),
     )(
         conserved.reshape(5, cj * ck, ni),

time: 68.1 us -> 61.1 us (0.90)
  local copies, waits for them, and re-layouts: 9.98 us -> 2.87 us
    unnamed x22 -> x4, local copies, waits for them, and re-layouts: 9.98 us -> 2.87 us
where the time goes in v1:
time: 61.1 us; the launch traced here: 60.9 us
  Pallas kernels  57.4 us (94%)
  local copies, waits for them, and re-layouts  2.87 us (5%)
  between operations  0.65 us (1%)
    pallas_call x1, Pallas kernels, body(): pl.pallas_call(functools.partial(kernel, nja, nka), out_shape=(flat, flat...  57.4 us
    unnamed x4, local copies, waits for them, and re-layouts  2.87 us

profile of v1, /device:TPU:29, one launch (start us, length us, event | category | flops | bytes accessed | tf_op | source)
XLA Modules:
  0.0 60.9 jit_solution(17026006623523288531)
XLA Ops:
  0.6 57.4 %shard_map.113 = (f32[5,256,128]{2,1,0:T(8,128)}, f32[5,256,128]{2,1,0:T(8,128)}) custom-call(f32[5,256,128]{2,1,0:T(8,128)} %bitcast.4, s32[256,128]{1,0:T(8,128)} %bitcast.7, s32[32,128]{1,0:T(8,128)} %refs_2_.1, f32[5,5]{1,0:T(8,128)} %refs_3_.1, f32[5,5]{1,0:T(8,128)} %refs_4_.1, f32[5,5]{1,0:T(8,128)} %refs_5_.1, f32[5,5]{1,0:T(8,128)} %refs_6_.1, ...), custom_call_target="tpu_custom_call" | custom-call | tf_op jit(solution)/shard_map/pallas_call | solution.py:466
  58.0 0.0 copy-start
  58.1 2.0 %copy.14 = f32[5,32,8,128]{3,2,1,0:T(8,128)} copy(f32[5,32,8,128]{3,2,1,0:T(8,128)} %bitcast.6) | data formatting | bytes 1310720
  60.1 0.0 copy-done
  60.1 0.8 %copy.15 = f32[5,32,8,128]{3,2,1,0:T(8,128)} copy(f32[5,32,8,128]{3,2,1,0:T(8,128)S(1)} %bitcast.5) | data formatting | bytes 1310720
Async XLA Ops:
  58.0 2.0 %copy-start = (f32[5,256,128]{2,1,0:T(8,128)S(1)}, f32[5,256,128]{2,1,0:T(8,128)}, u32[]{:S(2)}) copy-start(f32[5,256,128]{2,1,0:T(8,128)} %get-tuple-element.5) | copy-start | bytes 1966084

commit v2 on v1

--- a/solution.py
+++ b/solution.py
@@ -67,32 +67,32 @@
         normal_inverse,
     ) = inputs
     (
-    q,
-    jhalo,
-    first,
-    asend,
-    x,
-    solved,
-    bsend,
-    y,
-    w,
-    z,
-    normal,
-    csend,
-    u,
-    around3,
-    axial3,
-    normal3,
-    jsem,
-    ksem,
-    a_send,
-    a_recv,
-    b_send,
-    b_recv,
-    w_send,
-    w_recv,
-    c_send,
-    c_recv,
+        q,
+        jhalo,
+        first,
+        asend,
+        x,
+        solved,
+        bsend,
+        y,
+        w,
+        z,
+        normal,
+        csend,
+        u,
+        around3,
+        axial3,
+        normal3,
+        jsem,
+        ksem,
+        a_send,
+        a_recv,
+        b_send,
+        b_recv,
+        w_send,
+        w_recv,
+        c_send,
+        c_recv,
         insem,
     ) = refs
     loads = [
@@ -206,7 +206,12 @@
     for c in range(5):
         high, low = halves(around_inverse[c])
         around3[c] = jnp.concatenate([high, low, high], axis=1)
-        high, low = halves(axial_inverse[c])
+        rows = [
+            axial_inverse[c, pl.ds(p * cj + s, nka, stride=jq), :]
+            for p in range(nja)
+            for s in range(jq)
+        ]
+        high, low = halves(jnp.concatenate(rows, axis=0))
         axial3[c] = jnp.concatenate([high, high, low], axis=1)
         high, low = halves(normal_inverse[c])
         normal3[c] = jnp.concatenate([high, high, low], axis=1)
@@ -330,92 +335,90 @@
         for s in range(kp):
             solved[c, s] = out[:, s * ni : (s + 1) * ni]
 
-    def b_copy(dest, source):
+    def b_copy(dest, source, s):
         return pltpu.make_async_remote_copy(
-            src_ref=bsend.at[dest],
-            dst_ref=y.at[:, pl.ds(pl.multiple_of(source * (kp * cj), 8), kp * cj), :],
-            send_sem=b_send.at[dest],
-            recv_sem=b_recv.at[source],
+            src_ref=bsend.at[dest, s],
+            dst_ref=y.at[s, :, pl.ds(pl.multiple_of(source * (kp * nka), 8), kp * nka), :],
+            send_sem=b_send.at[dest, s],
+            recv_sem=b_recv.at[source, s],
             device_id={"ja": dest},
             device_id_type=MESH,
         )
 
-    for o in range(1, nja + 1):
-        dest = lax.rem(mj + o, nja)
-        for s in range(kp):
-            block = [
-                solved[c, s, pl.ds(pl.multiple_of(dest * cj, 8), cj), :] for c in range(5)
-            ]
-            block = mix(axial_to_normal, block)
+    for s in range(jq):
+        for o in range(1, nja + 1):
+            dest = lax.rem(mj + o, nja)
+            for t in range(kp):
+                rows = pl.ds(pl.multiple_of(dest * cj + s * nka, 8), nka)
+                block = mix(axial_to_normal, [solved[c, t, rows, :] for c in range(5)])
+                for c in range(5):
+                    if o < nja:
+                        bsend[dest, s, c, t * nka : (t + 1) * nka, :] = block[c]
+                    else:
+                        rows = pl.ds(pl.multiple_of((mj * kp + t) * nka, 8), nka)
+                        y[s, c, rows, :] = block[c]
+            if o < nja:
+                b_copy(dest, mj, s).start()
+
+    def w_copy(dest, source, s):
+        return pltpu.make_async_remote_copy(
+            src_ref=w.at[dest, s],
+            dst_ref=z.at[s, :, pl.ds(pl.multiple_of(source * ck, 8), ck), :],
+            send_sem=w_send.at[dest, s],
+            recv_sem=w_recv.at[source, s],
+            device_id={"ka": dest},
+            device_id_type=MESH,
+        )
+
+    for s in range(jq):
+        for o in range(1, nja):
+            source = lax.rem(mj + o, nja)
+            b_copy(source, source, s).wait_recv()
+        for o in range(1, nka + 1):
+            dest = lax.rem(mk + o, nka)
             for c in range(5):
-                if o < nja:
-                    bsend[dest, c, s * cj : (s + 1) * cj, :] = block[c]
+                tile = y[s, c, pl.ds(dest, ck, stride=nka), :]
+                if o < nka:
+                    w[dest, s, c] = tile
                 else:
-                    y[c, pl.ds(pl.multiple_of((mj * kp + s) * cj, 8), cj), :] = block[c]
-        if o < nja:
-            b_copy(dest, mj).start()
-    for o in range(1, nja):
-        source = lax.rem(mj + o, nja)
-        b_copy(source, source).wait_recv()
-
-    def w_copy(dest, source):
+                    z[s, c, pl.ds(pl.multiple_of(mk * ck, 8), ck), :] = tile
+            if o < nka:
+                w_copy(dest, mk, s).start()
+
+    def c_copy(dest, source, s):
         return pltpu.make_async_remote_copy(
-            src_ref=w.at[dest],
-            dst_ref=z.at[:, :, pl.ds(pl.multiple_of(source * ck, 8), ck), :],
-            send_sem=w_send.at[dest],
-            recv_sem=w_recv.at[source],
+            src_ref=csend.at[dest, s],
+            dst_ref=u.at[:, pl.ds(pl.multiple_of((source * jq + s) * ck, 8), ck), :],
+            send_sem=c_send.at[dest, s],
+            recv_sem=c_recv.at[source, s],
             device_id={"ka": dest},
             device_id_type=MESH,
         )
 
-    for o in range(1, nka + 1):
-        dest = lax.rem(mk + o, nka)
-        for s in range(jq):
-            for c in range(5):
-                tile = y[c, pl.ds(dest * jq + s, ck, stride=cj), :]
-                if o < nka:
-                    w[dest, c, s] = tile
-                else:
-                    z[c, s, pl.ds(pl.multiple_of(mk * ck, 8), ck), :] = tile
-        if o < nka:
-            w_copy(dest, mk).start()
-    for o in range(1, nka):
-        source = lax.rem(mk + o, nka)
-        w_copy(source, source).wait_recv()
-
-    for c in range(5):
-        high, low = halves(jnp.concatenate([z[c, s] for s in range(jq)], axis=1))
-        out = dot(normal3[c], jnp.concatenate([high, low, high], axis=0), ((1,), (0,)))
-        for s in range(jq):
-            normal[c, s] = out[:, s * ni : (s + 1) * ni]
-
-    def c_copy(dest, source):
-        return pltpu.make_async_remote_copy(
-            src_ref=csend.at[dest],
-            dst_ref=u.at[:, pl.ds(pl.multiple_of(source * (jq * ck), 8), jq * ck), :],
-            send_sem=c_send.at[dest],
-            recv_sem=c_recv.at[source],
-            device_id={"ka": dest},
-            device_id_type=MESH,
-        )
-
-    for o in range(1, nka + 1):
-        dest = lax.rem(mk + o, nka)
-        for s in range(jq):
-            block = [
-                normal[c, s, pl.ds(pl.multiple_of(dest * ck, 8), ck), :] for c in range(5)
-            ]
-            block = mix(char_back, block)
+    for s in range(jq):
+        for o in range(1, nka):
+            source = lax.rem(mk + o, nka)
+            w_copy(source, source, s).wait_recv()
+        for c in range(5):
+            high, low = halves(z[s, c])
+            normal[s, c] = dot(
+                normal3[c], jnp.concatenate([high, low, high], axis=0), ((1,), (0,))
+            )
+        for o in range(1, nka + 1):
+            dest = lax.rem(mk + o, nka)
+            rows = pl.ds(pl.multiple_of(dest * ck, 8), ck)
+            block = mix(char_back, [normal[s, c, rows, :] for c in range(5)])
             for c in range(5):
                 if o < nka:
-                    csend[dest, c, s * ck : (s + 1) * ck, :] = block[c]
+                    csend[dest, s, c] = block[c]
                 else:
                     u[c, pl.ds(pl.multiple_of((mk * jq + s) * ck, 8), ck), :] = block[c]
-        if o < nka:
-            c_copy(dest, mk).start()
-    for o in range(1, nka):
-        source = lax.rem(mk + o, nka)
-        c_copy(source, source).wait_recv()
+            if o < nka:
+                c_copy(dest, mk, s).start()
+    for s in range(jq):
+        for o in range(1, nka):
+            source = lax.rem(mk + o, nka)
+            c_copy(source, source, s).wait_recv()
 
     weight = blanking[...].astype(F32)
     for c in range(5):
@@ -436,11 +439,13 @@
     for o in range(1, nja):
         other = lax.rem(mj + o, nja)
         a_copy(other).wait_send()
-        b_copy(other, mj).wait_send()
+        for s in range(jq):
+            b_copy(other, mj, s).wait_send()
     for o in range(1, nka):
         other = lax.rem(mk + o, nka)
-        w_copy(other, mk).wait_send()
-        c_copy(other, mk).wait_send()
+        for s in range(jq):
+            w_copy(other, mk, s).wait_send()
+            c_copy(other, mk, s).wait_send()
 
 
 def body(
@@ -485,12 +490,12 @@
             pltpu.VMEM((nja, 5, kp, cj, ni), F32),
             pltpu.VMEM((5, kp, nj, ni), F32),
             pltpu.VMEM((5, kp, nj, ni), F32),
-            pltpu.VMEM((nja, 5, kp * cj, ni), F32),
-            pltpu.VMEM((5, ck * cj, ni), F32),
-            pltpu.VMEM((nka, 5, jq, ck, ni), F32),
-            pltpu.VMEM((5, jq, nk, ni), F32),
-            pltpu.VMEM((5, jq, nk, ni), F32),
-            pltpu.VMEM((nka, 5, jq * ck, ni), F32),
+            pltpu.VMEM((nja, jq, 5, kp * nka, ni), F32),
+            pltpu.VMEM((jq, 5, ck * nka, ni), F32),
+            pltpu.VMEM((nka, jq, 5, ck, ni), F32),
+            pltpu.VMEM((jq, 5, nk, ni), F32),
+            pltpu.VMEM((jq, 5, nk, ni), F32),
+            pltpu.VMEM((nka, jq, 5, ck, ni), F32),
             pltpu.VMEM((5, cj * ck, ni), F32),
             pltpu.VMEM((5, ni, 3 * ni), BF16),
             pltpu.VMEM((5, nj, 3 * nj), BF16),
@@ -499,12 +504,12 @@
             dma((2, 2)),
             dma((nja,)),
             dma((nja,)),
-            dma((nja,)),
-            dma((nja,)),
-            dma((nka,)),
-            dma((nka,)),
-            dma((nka,)),
-            dma((nka,)),
+            dma((nja, jq)),
+            dma((nja, jq)),
+            dma((nka, jq)),
+            dma((nka, jq)),
+            dma((nka, jq)),
+            dma((nka, jq)),
             dma((10,)),
         ],
         compiler_params=pltpu.CompilerParams(

time: 61.1 us -> 60.4 us (0.989)
  the two profiles are of different devices: /device:TPU:29 before, /device:TPU:0 now
where the time goes in v2:
time: 60.4 us; the launch traced here: 60.3 us
  Pallas kernels  56.8 us (94%)
  local copies, waits for them, and re-layouts  2.87 us (5%)
  between operations  0.65 us (1%)
    pallas_call x1, Pallas kernels, body(): pl.pallas_call(functools.partial(kernel, nja, nka), out_shape=(flat, flat...  56.8 us
    unnamed x4, local copies, waits for them, and re-layouts  2.87 us

profile of v2, /device:TPU:0, one launch (start us, length us, event | category | flops | bytes accessed | tf_op | source)
XLA Modules:
  0.0 60.3 jit_solution(4300488907494053765)
XLA Ops:
  0.6 56.8 %shard_map.113 = (f32[5,256,128]{2,1,0:T(8,128)}, f32[5,256,128]{2,1,0:T(8,128)}) custom-call(f32[5,256,128]{2,1,0:T(8,128)} %bitcast.4, s32[256,128]{1,0:T(8,128)} %bitcast.7, s32[32,128]{1,0:T(8,128)} %refs_2_.1, f32[5,5]{1,0:T(8,128)} %refs_3_.1, f32[5,5]{1,0:T(8,128)} %refs_4_.1, f32[5,5]{1,0:T(8,128)} %refs_5_.1, f32[5,5]{1,0:T(8,128)} %refs_6_.1, ...), custom_call_target="tpu_custom_call" | custom-call | tf_op jit(solution)/shard_map/pallas_call | solution.py:471
  57.4 0.0 copy-start
  57.4 2.0 %copy.14 = f32[5,32,8,128]{3,2,1,0:T(8,128)} copy(f32[5,32,8,128]{3,2,1,0:T(8,128)} %bitcast.6) | data formatting | bytes 1310720
  59.4 0.0 copy-done
  59.4 0.8 %copy.15 = f32[5,32,8,128]{3,2,1,0:T(8,128)} copy(f32[5,32,8,128]{3,2,1,0:T(8,128)S(1)} %bitcast.5) | data formatting | bytes 1310720
Async XLA Ops:
  57.4 2.0 %copy-start = (f32[5,256,128]{2,1,0:T(8,128)S(1)}, f32[5,256,128]{2,1,0:T(8,128)}, u32[]{:S(2)}) copy-start(f32[5,256,128]{2,1,0:T(8,128)} %get-tuple-element.5) | copy-start | bytes 1966084

commit v3 on v2

--- a/solution.py
+++ b/solution.py
@@ -52,8 +52,8 @@
     *refs,
 ):
     sources, refs = refs[:10], refs[10:]
-    right_side, update = refs[:2]
-    inputs, refs = refs[2:12], refs[12:]
+    right_side, update, active = refs[:3]
+    inputs, refs = refs[3:13], refs[13:]
     (
         cells,
         blanking,
@@ -259,11 +259,11 @@
             above, below = reader(2), reader(-2)
             for c in range(5):
                 total[c] = total[c] + (above[c] + below[c]) * (1.0 / 32.0)
-        weight = -0.5 * blanking[pl.ds(k, cj, stride=ck), :].astype(F32)
+        weight = blanking[pl.ds(k, cj, stride=ck), :].astype(F32)
         total = [t * weight for t in total]
         for c in range(5):
             right_side[c, pl.ds(k, cj, stride=ck), :] = total[c]
-        mixed = mix(char_around, total)
+        mixed = mix(char_around, [-0.5 * t for t in total])
         for c in range(5):
             first[c, k] = mixed[c]
         return carry
@@ -420,9 +420,9 @@
             source = lax.rem(mk + o, nka)
             c_copy(source, source, s).wait_recv()
 
-    weight = blanking[...].astype(F32)
+    active[...] = blanking[...].astype(F32)
     for c in range(5):
-        update[c] = u[c] * weight
+        update[c] = u[c]
 
     for upward, last, here in ((True, nja - 1, mj), (False, 0, mj)):
 
@@ -468,11 +468,11 @@
     vmem = pl.BlockSpec(memory_space=pltpu.VMEM)
     flat = jax.ShapeDtypeStruct((5, cj * ck, ni), F32)
     dma = pltpu.SemaphoreType.DMA
-    right_side, update = pl.pallas_call(
+    right_side, update, active = pl.pallas_call(
         functools.partial(kernel, nja, nka),
-        out_shape=(flat, flat),
+        out_shape=(flat, flat, jax.ShapeDtypeStruct((cj * ck, ni), F32)),
         in_specs=[pl.BlockSpec(memory_space=pltpu.HBM)] * 10,
-        out_specs=(vmem, vmem),
+        out_specs=(vmem, vmem, vmem),
         scratch_shapes=[
             pltpu.VMEM((5, cj * ck, ni), F32),
             pltpu.VMEM((cj * ck, ni), jnp.int32),
@@ -527,6 +527,7 @@
         axial_inverse,
         normal_inverse,
     )
+    right_side, update = -0.5 * right_side, update * active
     return right_side.reshape(conserved.shape), update.reshape(conserved.shape)
 
 

time: 60.4 us -> 60.1 us (level)
  local copies, waits for them, and re-layouts: 2.87 us -> 0 us
  other arithmetic: 0 us -> 2.51 us
    unnamed x4 -> x0, local copies, waits for them, and re-layouts: 2.87 us -> none
    reshape x0 -> x1, other arithmetic: none -> 2.51 us  [body(): update.reshape(conserved.shape)]
where the time goes in v3:
time: 60.1 us; the launch traced here: 60 us
  Pallas kernels  56.8 us (95%)
  other arithmetic  2.51 us (4%)
  between operations  0.64 us (1%)
    pallas_call x1, Pallas kernels, body(): pl.pallas_call(functools.partial(kernel, nja, nka), out_shape=(flat, flat...  56.8 us
    reshape x1, other arithmetic, body(): update.reshape(conserved.shape)  2.51 us

profile of v3, /device:TPU:0, one launch (start us, length us, event | category | flops | bytes accessed | tf_op | source)
XLA Modules:
  0.0 60.0 jit_solution(8824191092602503610)
XLA Ops:
  0.6 56.8 %shard_map.113 = (f32[5,256,128]{2,1,0:T(8,128)}, f32[5,256,128]{2,1,0:T(8,128)}, f32[256,128]{1,0:T(8,128)}) custom-call(f32[5,256,128]{2,1,0:T(8,128)} %bitcast.6, s32[256,128]{1,0:T(8,128)} %bitcast.7, s32[32,128]{1,0:T(8,128)} %refs_2_.1, f32[5,5]{1,0:T(8,128)} %refs_3_.1, f32[5,5]{1,0:T(8,128)} %refs_4_.1, f32[5,5]{1,0:T(8,128)} %refs_5_.1, ...), custom_call_target="tpu_custom_call" | custom-call | tf_op jit(solution)/shard_map/pallas_call | solution.py:471
  57.5 2.5 %multiply_bitcast_fusion = (f32[5,32,8,128]{3,2,1,0:T(8,128)}, f32[5,32,8,128]{3,2,1,0:T(8,128)}) fusion(f32[5,256,128]{2,1,0:T(8,128)} %get-tuple-element.6, f32[256,128]{1,0:T(8,128)} %get-tuple-element.7, f32[5,256,128]{2,1,0:T(8,128)} %get-tuple-element.5), kind=kLoop, calls=%fused_computation | loop fusion | flops 327680 | bytes 2752512 | tf_op jit(solution)/shard_map/reshape | solution.py:531
